TPU v7x, 32 devices: a whole 2x2x4 slice. The times are simulated.
32 devices in a mesh: grp: 2 (over y), row: 4 (over z), sub: 4 (over x, core).
Axes of the slice: x: 2, y: 2, z: 4, core: 2. Of those that a mesh axis runs over, the one named last changes fastest.
Arguments:
- observed: float32 [512, 128], P(('grp', 'row')), parts along dimension 0, may hold values from -18 to 18
- sens_tiles: bfloat16 [8, 4, 128, 64, 128], P(('grp', 'row'), 'sub'), parts along dimension 0, may hold values from -0.25 to 0.25
- tile_row: int32 [8, 4, 128], P(('grp', 'row'), 'sub'), parts along dimension 0, may hold values from 0 to 63
- tile_owner: int32 [8, 4, 128], P(('grp', 'row'), 'sub'), parts along dimension 0, may hold values from 0 to 3, as said below
- tile_block: int32 [8, 4, 128], P(('grp', 'row'), 'sub'), parts along dimension 0, may hold values from 0 to 1023
- coeffs: float32 [512, 64, 64], P(('grp', 'row'), 'sub'), parts along dimension 0, may hold values from -6 to 6
- split_var: float32 [128, 64, 256], P(('grp', 'row'), 'sub'), parts along dimension 0, may hold values from -3.15 to 3.15, as said below
- scaled_dual: float32 [128, 64, 256], P(('grp', 'row'), 'sub'), parts along dimension 0, may hold values from -16.2 to 16.2
- lower_bound: float32 [128, 64, 256], P(('grp', 'row'), 'sub'), parts along dimension 0, may hold values from -10.8 to -0.4
- upper_bound: float32 [128, 64, 256], P(('grp', 'row'), 'sub'), parts along dimension 0, may hold values from 0.4 to 10.8
Outputs:
- model_next: float32 [128, 64, 256], P(('grp', 'row'), 'sub'), parts along dimension 0
- split_next: float32 [128, 64, 256], P(('grp', 'row'), 'sub'), parts along dimension 0
- dual_next: float32 [128, 64, 256], P(('grp', 'row'), 'sub'), parts along dimension 0
- residual_norms: float32 [6], P('grp'), parts along dimension 0
There are 2 independent parts, one for each index of `grp`. A program takes and returns all parts, laid end to end along the dimension named above; each array names one. Nothing has to cross between parts.
Inputs may be any that keep to these rules, and one draw needn't show every extreme that they name: `tile_owner`: within one device's list (fixed r and s), at most 96 tiles name the same owner row; in each sub column one owner row is named exactly 96 times in every device's list. lower_bound <= split_var <= upper_bound in every cell.
All inputs are finite; a program needn't handle non-finite values.
Results may differ from a plain program's by a relative error of at most 0.0028.
Values may be sent and summed in bfloat16 or wider, within the bound.
A program may use at most 64 MiB of HBM per device.

v0:
```python
import jax
import jax.numpy as jnp
from jax import lax
from jax.sharding import PartitionSpec as P

LEVELS = 3


half_root = 0.7071067811865476
step_size = 0.1
smooth_weight = 0.5
data_weight = 20.0
penalty = 1.0


def padded_2(cells, sides, width):
    for axis, dim in sides:
        count = lax.axis_size(axis)
        ends = count - 1
        head = lax.slice_in_dim(cells, 0, width, axis=dim)
        tail = lax.slice_in_dim(cells, cells.shape[dim] - width, cells.shape[dim], axis=dim)
        cells = jnp.concatenate(
            [
                lax.ppermute(tail, axis, [(i, (i + 1) % count) for i in range(ends)]),
                cells,
                lax.ppermute(head, axis, [((i + 1) % count, i) for i in range(ends)]),
            ],
            axis=dim,
        )
    return cells


def synthesis(coef_field):
    total_len = coef_field.shape[-1]
    band_len = total_len >> LEVELS
    approx = coef_field[..., :band_len]
    for level_idx in range(LEVELS):
        detail = coef_field[..., band_len : 2 * band_len]
        paired = jnp.stack(((approx + detail) * half_root, (approx - detail) * half_root), axis=-1)
        approx = paired.reshape(coef_field.shape[:-1] + (2 * band_len,))
        band_len = 2 * band_len
    return approx


def haar_table(length_all):
    return synthesis(jnp.eye(length_all, dtype=jnp.float32))


def body(
    observed,
    sens_tiles,
    tile_row,
    tile_owner,
    tile_block,
    coeffs,
    split_var,
    scaled_dual,
    lower_bound,
    upper_bound,
):
    row_count = lax.axis_size("row")
    sub_count = lax.axis_size("sub")
    tile_mats = sens_tiles[0, 0]
    row_ids = tile_row[0, 0]
    owner_ids = tile_owner[0, 0]
    block_idx = tile_block[0, 0]
    tile_count = tile_mats.shape[0]
    block_width = tile_mats.shape[1]
    row_blocks = observed.shape[0]
    block_total = coeffs.size // block_width
    capacity = 3 * tile_count // row_count
    slot_total = row_count * capacity
    local_blocks = coeffs.astype(jnp.bfloat16).reshape(block_total, block_width)
    owner_hot = (owner_ids[:, None] == jnp.arange(row_count, dtype=jnp.int32)[None, :]).astype(
        jnp.int32
    )
    slot_ids = jnp.sum((jnp.cumsum(owner_hot, axis=0) - owner_hot) * owner_hot, axis=1)
    flat_slot = owner_ids * capacity + slot_ids
    slot_match = flat_slot[None, :] == jnp.arange(slot_total, dtype=jnp.int32)[:, None]
    requests = jnp.sum(jnp.where(slot_match, block_idx[None, :], 0), axis=1).reshape(
        row_count, capacity
    )
    asked_ids = lax.all_to_all(requests, "row", split_axis=0, concat_axis=0, tiled=True)
    values = local_blocks[asked_ids.reshape(-1)].reshape(
        asked_ids.shape[0], asked_ids.shape[1] * block_width
    )
    returned = lax.all_to_all(values, "row", split_axis=0, concat_axis=0, tiled=True)
    fetched = returned.reshape(asked_ids.shape[0], asked_ids.shape[1], block_width)
    picked = fetched[owner_ids, slot_ids]
    partial_rows = jnp.einsum("tk,tki->ti", picked, tile_mats, preferred_element_type=jnp.float32)
    row_hot = (row_ids[:, None] == jnp.arange(row_blocks, dtype=jnp.int32)[None, :]).astype(
        jnp.float32
    )
    pred_part = jnp.einsum("tb,ti->bi", row_hot, partial_rows, precision=lax.Precision.HIGHEST)
    share_rows = row_blocks // sub_count
    share_start = lax.axis_index("sub") * share_rows
    predicted = lax.psum(pred_part, "sub")
    residual = predicted - observed
    resid_low = residual.astype(jnp.bfloat16)
    own_resid = lax.dynamic_slice_in_dim(residual, share_start, share_rows, 0)
    data_count = row_blocks * observed.shape[1] * row_count
    misfit_part = 0.5 * jnp.sum(own_resid * own_resid) / data_count
    misfit = lax.psum(misfit_part, ("row", "sub"))
    resid_tiles = resid_low[row_ids]
    contrib = jnp.einsum("tki,ti->tk", tile_mats, resid_tiles, preferred_element_type=jnp.float32)
    placing = slot_match.astype(jnp.float32)
    outgoing = jnp.dot(placing, contrib, precision=lax.Precision.HIGHEST)
    incoming = lax.all_to_all(
        outgoing.reshape(row_count, capacity * block_width),
        "row",
        split_axis=0,
        concat_axis=0,
        tiled=True,
    )
    taking = (
        asked_ids.reshape(-1)[None, :] == jnp.arange(block_total, dtype=jnp.int32)[:, None]
    ).astype(jnp.float32)
    grad_blocks = jnp.dot(
        taking, incoming.reshape(slot_total, block_width), precision=lax.Precision.HIGHEST
    )
    coef_grad = grad_blocks.reshape(coeffs.shape)
    first_table = haar_table(coeffs.shape[2])
    depth_table = haar_table(coeffs.shape[0] * row_count)
    along_model = jnp.dot(coeffs, first_table, precision=lax.Precision.HIGHEST)
    along_grad = jnp.dot(coef_grad, first_table, precision=lax.Precision.HIGHEST)
    part_list = (
        lax.all_to_all(along_model, "row", split_axis=2, concat_axis=0, tiled=True),
        lax.all_to_all(along_grad, "row", split_axis=2, concat_axis=0, tiled=True),
    )
    model_now, descent = tuple(
        (
            jnp.einsum("zyx,zw->xyw", slab_part, depth_table, precision=lax.Precision.HIGHEST)
            for slab_part in part_list
        )
    )
    padded = padded_2(model_now.astype(jnp.bfloat16), (("row", 0), ("sub", 1)), 1).astype(
        model_now.dtype
    )
    depth_pad = jnp.pad(model_now, ((0, 0), (0, 0), (1, 1)))
    beside = padded[2:, 1:-1, :] + padded[:-2, 1:-1, :]
    beside = beside + padded[1:-1, 2:, :] + padded[1:-1, :-2, :]
    beside = beside + depth_pad[:, :, 2:] + depth_pad[:, :, :-2]
    smooth = 6.0 * model_now - beside
    model_next = model_now - step_size * (
        data_weight * descent
        + smooth_weight * smooth
        + penalty * (model_now - split_var + scaled_dual)
    )
    split_next = jnp.clip(model_next + scaled_dual, lower_bound, upper_bound)
    dual_next = scaled_dual + model_next - split_next
    cell_total = model_now.size * row_count * sub_count
    primal_gap = model_next - split_next
    dual_gap = split_next - split_var
    primal_part = jnp.sum(primal_gap * primal_gap) / cell_total
    dual_part = jnp.sum(dual_gap * dual_gap) / cell_total
    primal_sum, dual_sum = lax.psum((primal_part, dual_part), ("row", "sub"))
    residual_norms = jnp.stack([misfit, jnp.sqrt(primal_sum), penalty * jnp.sqrt(dual_sum)])
    return (model_next, split_next, dual_next, residual_norms)


def solution(mesh):
    in_specs = (
        P(("grp", "row"), None),
        P(("grp", "row"), "sub", None, None, None),
        P(("grp", "row"), "sub", None),
        P(("grp", "row"), "sub", None),
        P(("grp", "row"), "sub", None),
        P(("grp", "row"), "sub", None),
        P(("grp", "row"), "sub", None),
        P(("grp", "row"), "sub", None),
        P(("grp", "row"), "sub", None),
        P(("grp", "row"), "sub", None),
    )
    out_specs = (
        P(("grp", "row"), "sub", None),
        P(("grp", "row"), "sub", None),
        P(("grp", "row"), "sub", None),
        P("grp"),
    )
    return jax.shard_map(body, mesh=mesh, in_specs=in_specs, out_specs=out_specs, check_vma=False)
```

profile of v0, /device:TPU:0, one launch (start us, length us, event | category | flops | bytes accessed | tf_op | source)
XLA Modules:
  0.0 141.9 jit_solution(10157898567690040231)
XLA Ops:
  0.7 0.9 fusion.24
  1.7 0.8 select_reduce_fusion.1
  2.6 0.7 multiply_add_fusion.1
  3.2 0.8 select_reduce_fusion
  4.0 0.7 all_to_all.48
  4.7 6.3 %all-to-all-start.1 = ((s32[4,1,96]{2,1,0:T(1,128)}), s32[4,1,96]{2,1,0:T(1,128)S(1)}, u32[]{:S(2)}, u32[]{:S(2)}) async-start(s32[4,1,96]{2,1,0:T(1,128)} %all_to_all.48), calls=%async_computation.1 | async-start | bytes 4096 | tf_op jit(solution)/shard_map/all_to_all | solution.py:83
  11.0 0.7 fusion.35
  12.2 0.7 multiply_bitcast_fusion.1
  13.0 1.7 %convolution_bitcast_fusion = f32[64,16,64]{0,2,1:T(8,128)S(1)} fusion(f32[64,64,1]{0,1,2:T(8,128)S(1)} %bitcast.117, f32[64,16,64]{2,1,0:T(8,128)S(1)} %copy-done.1), kind=kOutput, calls=%fused_computation.9 | convolution fusion | flops 50331648 | bytes 540672 | tf_op jit(solution)/shard_map/dot_general | solution.py:124
  14.6 0.5 fusion.34
  15.2 1.3 all-to-all-done.1
  16.6 1.4 %gather_fusion = bf16[384,64]{1,0:T(8,128)(2,1)S(1)} fusion(bf16[1024,64]{1,0:T(8,128)(2,1)S(1)} %bitcast.109, s32[1024]{0:T(1024)S(1)} %pad_clamp_fusion.1), kind=kCustom, calls=%fused_computation | custom fusion | bytes 99840 | tf_op jit(solution)/shard_map/gather | solution.py:84
  18.2 0.5 broadcast.172
  18.7 0.9 reduce.11
  19.6 0.7 reshape.244
  20.3 3.8 %all-to-all-start.2 = ((bf16[4,2,3072]{2,1,0:T(2,128)(2,1)}), bf16[4,2,3072]{2,1,0:T(2,128)(2,1)S(1)}, u32[]{:S(2)}, u32[]{:S(2)}) async-start(bf16[4,2,3072]{2,1,0:T(2,128)(2,1)} %reshape.244), calls=%async_computation.2 | async-start | bytes 98304 | tf_op jit(solution)/shard_map/all_to_all | solution.py:87
  24.1 0.7 pad_clamp_fusion
  24.7 5.0 %all-to-all-done.2 = bf16[4,2,3072]{2,1,0:T(2,128)(2,1)S(1)} async-done(((bf16[4,2,3072]{2,1,0:T(2,128)(2,1)}), bf16[4,2,3072]{2,1,0:T(2,128)(2,1)S(1)}, u32[]{:S(2)}, u32[]{:S(2)}) %all-to-all-start.2) | async-done | bytes 49184 | tf_op jit(solution)/shard_map/all_to_all | solution.py:87
  29.8 0.3 reduce.3
  30.3 1.1 gather_fusion.1
  31.4 0.7 fusion.2
  32.0 0.3 fusion.25
  32.3 10.3 %psum.28 = f32[64,128]{1,0:T(8,128)S(1)} all-reduce(f32[64,128]{1,0:T(8,128)S(1)} %fusion.25), channel_id=1, replica_groups=mesh['grp'=2,'row'=4,'sub'=4] {'sub'}, use_global_device_ids=true, to_apply=%region_3.4 | all-reduce | flops 8192 | bytes 65536 | tf_op jit(solution)/shard_map/psum | solution.py:97
  42.6 0.6 fusion.37
  43.3 0.7 gather_fusion.2
  44.0 1.2 fusion
  45.4 0.8 all_to_all.59
  46.2 3.3 %all-to-all-start.3 = ((f32[4,1,6144]{2,1,0:T(1,128)}), f32[4,1,6144]{2,1,0:T(1,128)S(1)}, u32[]{:S(2)}, u32[]{:S(2)}) async-start(f32[4,1,6144]{2,1,0:T(1,128)} %all_to_all.59), calls=%async_computation.3 | async-start | bytes 196608 | tf_op jit(solution)/shard_map/all_to_all | solution.py:108
  50.0 1.1 copy.157
  51.1 2.1 %reshape.242 = f32[4,1,16384]{2,1,0:T(1,128)} reshape(f32[64,16,64]{2,1,0:T(8,128)} %bitcast.111) | data formatting | bytes 524288
  53.1 0.5 broadcast.170
  53.6 0.7 reduce.9
  54.4 1.1 all-to-all-done.3
  55.5 4.0 %all-to-all-start = ((f32[4,1,16384]{2,1,0:T(1,128)}), f32[4,1,16384]{2,1,0:T(1,128)}, u32[]{:S(2)}, u32[]{:S(2)}) async-start(f32[4,1,16384]{2,1,0:T(1,128)} %reshape.242), calls=%async_computation | async-start | bytes 524288 | tf_op jit(solution)/shard_map/all_to_all | solution.py:127
  59.9 0.9 fusion.4
  60.8 0.6 fusion.40
  61.4 0.3 copy.105
  61.7 1.0 reshape.246
  62.7 5.8 %all-to-all-done = f32[4,1,16384]{2,1,0:T(1,128)} async-done(((f32[4,1,16384]{2,1,0:T(1,128)}), f32[4,1,16384]{2,1,0:T(1,128)}, u32[]{:S(2)}, u32[]{:S(2)}) %all-to-all-start) | async-done | bytes 262176 | tf_op jit(solution)/shard_map/all_to_all | solution.py:127
  68.5 4.2 %all-to-all-start.4 = ((f32[4,1,16384]{2,1,0:T(1,128)}), f32[4,1,16384]{2,1,0:T(1,128)}, u32[]{:S(2)}, u32[]{:S(2)}) async-start(f32[4,1,16384]{2,1,0:T(1,128)} %reshape.246), calls=%async_computation.4 | async-start | bytes 524288 | tf_op jit(solution)/shard_map/all_to_all | solution.py:128
  72.7 0.5 broadcast.171
  73.2 2.3 %reduce.10 = f32[4,16384]{1,0:T(4,128)S(1)} reduce(f32[4,1,16384]{2,1,0:T(1,128)} %all-to-all-done, f32[]{:T(128)} %broadcast.171), dimensions={1}, to_apply=%all_to_all.44.reduce_sub_computation | reduce | bytes 524292 | tf_op jit(solution)/shard_map/all_to_all | solution.py:127
  75.5 0.3 reshape.243
  75.8 0.3 copy.156
  76.1 0.3 reshape.215
  76.5 0.4 fusion.39
  76.9 3.7 %collective-permute-start = (bf16[1,16,256]{2,0,1:T(2,128)(2,1)S(1)}, bf16[1,16,256]{2,0,1:T(2,128)(2,1)S(1)}, u32[]{:S(2)}, u32[]{:S(2)}) collective-permute-start(bf16[1,16,256]{2,0,1:T(2,128)(2,1)S(1)} %get-tuple-element.37), channel_id=1, source_target_pairs={{0,4},{4,8},{8,12},{1,5},{5,9},{9,13},{2,6},{6,10},{10,14},{3,7},{... | collective-permute-start | bytes 24584 | tf_op jit(solution)/shard_map/ppermute | solution.py:24
  80.7 1.3 collective-permute-start.1
  82.1 4.2 %collective-permute-done.1 = bf16[1,16,256]{2,0,1:T(2,128)(2,1)S(1)} collective-permute-done((bf16[1,16,256]{2,0,1:T(2,128)(2,1)S(1)}, bf16[1,16,256]{2,0,1:T(2,128)(2,1)S(1)}, u32[]{:S(2)}, u32[]{:S(2)}) %collective-permute-start.1) | collective-permute-done | bytes 8224 | tf_op jit(solution)/shard_map/ppermute | solution.py:26
  86.3 1.3 collective-permute-start.2
  87.6 1.3 collective-permute-start.3
  88.9 1.3 multiply_reduce_fusion.2
  90.9 1.1 collective-permute-done.3
  92.0 2.3 %reduce.12 = f32[4,16384]{1,0:T(4,128)S(1)} reduce(f32[4,1,16384]{2,1,0:T(1,128)} %all-to-all-done.4, f32[]{:T(128)} %broadcast.171), dimensions={1}, to_apply=%all_to_all.54.reduce_sub_computation | reduce | bytes 524292 | tf_op jit(solution)/shard_map/all_to_all | solution.py:128
  94.3 1.1 reshape.247
  95.4 2.2 %copy.107 = f32[4,64,16,16]{1,0,3,2:T(4,128)} copy(f32[4,64,16,16]{1,2,3,0:T(8,128)} %bitcast.115) | data formatting | bytes 524288 | tf_op jit(solution)/shard_map/all_to_all | solution.py:128
  97.6 1.4 reshape.223
  99.0 0.4 fusion.41
  99.4 2.6 %multiply_reduce_fusion.1 = (f32[]{:T(128)}, f32[]{:T(128)}, f32[16,16,256]{2,0,1:T(8,128)S(1)}, f32[16,16,256]{2,0,1:T(8,128)S(1)}) fusion(f32[16,16,256]{2,1,0:T(8,128)} %param.16, f32[16,16,256]{2,1,0:T(8,128)} %param.17, f32[16,16,256]{2,1,0:T(8,128)} %param.18, f32[16,16,256]{2,1,0:T(8,128)} %param.19, f32[16,16,256]{2,0,1:T(8,128)S(1)} %bitcast.110, ...), kind=kLoop, calls=%fused_computation.31 | loop fusion | flops 1572862 | bytes 3145736 | tf_op jit(solution)/shard_map/reduce_sum | solution.py:154
  102.0 0.9 copy.116
  103.0 0.9 copy.115
  105.2 33.2 %all-reduce.1 = (f32[]{:T(128)}, f32[]{:T(128)}, f32[1]{0:T(128)}) all-reduce(f32[]{:T(128)S(6)} %div.11, f32[]{:T(128)S(6)} %div.10, f32[1]{0:T(128)} %bitcast.46), channel_id=1, replica_groups=mesh['grp'=2,'row'=4,'sub'=4] {'row','sub'}, use_global_device_ids=true, to_apply=%region_9.10 | all-reduce | flops 3 | bytes 24 | tf_op jit(solution)/shard_map/psum | solution.py:156
  139.8 0.9 copy.117
  140.6 1.3 pad_maximum_fusion.9
  (58 shorter events, 2.7 us)
Async XLA Ops:
  0.6 30.8 %copy-start = (bf16[1,1,128,64,128]{4,3,2,1,0:T(8,128)(2,1)S(1)}, bf16[1,1,128,64,128]{4,3,2,1,0:T(8,128)(2,1)}, u32[]{:S(2)}) copy-start(bf16[1,1,128,64,128]{4,3,2,1,0:T(8,128)(2,1)} %param.11) | copy-start | bytes 6291460
  0.6 12.3 %copy-start.1 = (f32[64,16,64]{2,1,0:T(8,128)S(1)}, f32[64,16,64]{2,1,0:T(8,128)}, u32[]{:S(2)}) copy-start(f32[64,16,64]{2,1,0:T(8,128)} %param.15) | copy-start | bytes 786436
  0.7 14.0 %copy-start.7 = (s32[1,1,128]{2,1,0:T(1,128)S(1)}, s32[1,1,128]{2,1,0:T(1,128)}, u32[]{:S(2)}) copy-start(s32[1,1,128]{2,1,0:T(1,128)} %param.12) | copy-start | bytes 1540
  4.7 11.8 %all-to-all-start.1 = ((s32[4,1,96]{2,1,0:T(1,128)}), s32[4,1,96]{2,1,0:T(1,128)S(1)}, u32[]{:S(2)}, u32[]{:S(2)}) async-start(s32[4,1,96]{2,1,0:T(1,128)} %all_to_all.48), calls=%async_computation.1 | async-start | bytes 4096 | tf_op jit(solution)/shard_map/all_to_all | solution.py:83
  12.9 1.7 %copy-start.4 = (f32[64,32,2]{0,2,1:T(2,128)}, f32[64,32,2]{0,2,1:T(2,128)S(1)}, u32[]{:S(2)}) copy-start(f32[64,32,2]{0,2,1:T(2,128)S(1)} %pad_maximum_fusion.3) | copy-start | bytes 49156
  18.1 24.6 %copy-start.6 = (f32[64,128]{1,0:T(8,128)S(1)}, f32[64,128]{1,0:T(8,128)}, u32[]{:S(2)}) copy-start(f32[64,128]{1,0:T(8,128)} %param.10) | copy-start | bytes 98308
  20.3 9.5 %all-to-all-start.2 = ((bf16[4,2,3072]{2,1,0:T(2,128)(2,1)}), bf16[4,2,3072]{2,1,0:T(2,128)(2,1)S(1)}, u32[]{:S(2)}, u32[]{:S(2)}) async-start(bf16[4,2,3072]{2,1,0:T(2,128)(2,1)} %reshape.244), calls=%async_computation.2 | async-start | bytes 98304 | tf_op jit(solution)/shard_map/all_to_all | solution.py:87
  32.0 17.5 %copy-start.3 = (f32[256,128,1]{0,1,2:T(8,128)S(1)}, f32[256,128,1]{0,1,2:T(8,128)}, u32[]{:S(2)}) copy-start(f32[256,128,1]{0,1,2:T(8,128)} %get-tuple-element.30) | copy-start | bytes 393220
  46.2 9.3 %all-to-all-start.3 = ((f32[4,1,6144]{2,1,0:T(1,128)}), f32[4,1,6144]{2,1,0:T(1,128)S(1)}, u32[]{:S(2)}, u32[]{:S(2)}) async-start(f32[4,1,6144]{2,1,0:T(1,128)} %all_to_all.59), calls=%async_computation.3 | async-start | bytes 196608 | tf_op jit(solution)/shard_map/all_to_all | solution.py:108
  49.8 11.0 %copy-start.5 = (f32[64,32,2]{0,2,1:T(2,128)S(1)}, f32[64,32,2]{0,2,1:T(2,128)}, u32[]{:S(2)}) copy-start(f32[64,32,2]{0,2,1:T(2,128)} %copy-done.4) | copy-start | bytes 49156
  55.5 13.0 %all-to-all-start = ((f32[4,1,16384]{2,1,0:T(1,128)}), f32[4,1,16384]{2,1,0:T(1,128)}, u32[]{:S(2)}, u32[]{:S(2)}) async-start(f32[4,1,16384]{2,1,0:T(1,128)} %reshape.242), calls=%async_computation | async-start | bytes 524288 | tf_op jit(solution)/shard_map/all_to_all | solution.py:127
  68.5 23.6 %all-to-all-start.4 = ((f32[4,1,16384]{2,1,0:T(1,128)}), f32[4,1,16384]{2,1,0:T(1,128)}, u32[]{:S(2)}, u32[]{:S(2)}) async-start(f32[4,1,16384]{2,1,0:T(1,128)} %reshape.246), calls=%async_computation.4 | async-start | bytes 524288 | tf_op jit(solution)/shard_map/all_to_all | solution.py:128
  76.9 5.1 %collective-permute-start = (bf16[1,16,256]{2,0,1:T(2,128)(2,1)S(1)}, bf16[1,16,256]{2,0,1:T(2,128)(2,1)S(1)}, u32[]{:S(2)}, u32[]{:S(2)}) collective-permute-start(bf16[1,16,256]{2,0,1:T(2,128)(2,1)S(1)} %get-tuple-element.37), channel_id=1, source_target_pairs={{0,4},{4,8},{8,12},{1,5},{5,9},{9,13},{2,6},{6,10},{10,14},{3,7},{... | collective-permute-start | bytes 24584 | tf_op jit(solution)/shard_map/ppermute | solution.py:24
  80.7 5.6 %collective-permute-start.1 = (bf16[1,16,256]{2,0,1:T(2,128)(2,1)S(1)}, bf16[1,16,256]{2,0,1:T(2,128)(2,1)S(1)}, u32[]{:S(2)}, u32[]{:S(2)}) collective-permute-start(bf16[1,16,256]{2,0,1:T(2,128)(2,1)S(1)} %get-tuple-element.38), channel_id=1, source_target_pairs={{4,0},{8,4},{12,8},{5,1},{9,5},{13,9},{6,2},{10,6},{14,10},{7,3},{... | collective-permute-start | bytes 24584 | tf_op jit(solution)/shard_map/ppermute | solution.py:26
  86.3 4.6 %collective-permute-start.2 = (bf16[18,1,256]{2,0,1:T(8,128)(2,1)S(1)}, bf16[18,1,256]{2,0,1:T(8,128)(2,1)S(1)}, u32[]{:S(2)}, u32[]{:S(2)}) collective-permute-start(bf16[18,1,256]{2,0,1:T(8,128)(2,1)S(1)} %get-tuple-element.35), channel_id=1, source_target_pairs={{0,1},{1,2},{2,3},{4,5},{5,6},{6,7},{8,9},{9,10},{10,11},{12,13},{... | collective-permute-start | bytes 27656 | tf_op jit(solution)/shard_map/ppermute | solution.py:24
  87.6 4.4 %collective-permute-start.3 = (bf16[18,1,256]{2,0,1:T(8,128)(2,1)S(1)}, bf16[18,1,256]{2,0,1:T(8,128)(2,1)S(1)}, u32[]{:S(2)}, u32[]{:S(2)}) collective-permute-start(bf16[18,1,256]{2,0,1:T(8,128)(2,1)S(1)} %get-tuple-element.36), channel_id=1, source_target_pairs={{1,0},{2,1},{3,2},{5,4},{6,5},{7,6},{9,8},{10,9},{11,10},{13,12},{... | collective-permute-start | bytes 27656 | tf_op jit(solution)/shard_map/ppermute | solution.py:26
  99.0 3.9 %copy-start.2 = (f32[16,16,256]{2,1,0:T(8,128)S(1)}, f32[16,16,256]{2,1,0:T(8,128)}, u32[]{:S(2)}) copy-start(f32[16,16,256]{2,1,0:T(8,128)} %param.17) | copy-start | bytes 786436
where the time goes:
time: 143 us; the launch traced here: 142 us
  blocking collectives  43.4 us (30%)
  starting transfers between devices  29.3 us (20%)
  local copies, waits for them, and re-layouts  21 us (15%)
  other arithmetic  18.9 us (13%)
  waiting for transfers between devices  18.6 us (13%)
  matrix products  6.3 us (4%)
  between operations  4.45 us (3%)
    psum x1, blocking collectives, body(): primal_sum, dual_sum = lax.psum((primal_part, dual_part), ('row', 'sub'))  33.2 us
    psum x1, blocking collectives, body(): predicted = lax.psum(pred_part, 'sub')  10.3 us
    unnamed x27, local copies, waits for them, and re-layouts  9.49 us
    all_to_all x1, starting transfers between devices, body(): lax.all_to_all(requests, 'row', split_axis=0, concat_axis=0, tiled=True)  6.32 us
    all_to_all x1, waiting for transfers between devices, body(): lax.all_to_all(along_model, 'row', split_axis=2, concat_axis=0, tiled=True)  5.76 us
    ppermute x2, waiting for transfers between devices, padded_2(): lax.ppermute(head, axis, [((i + 1) % count, i) for i in range(ends)])  5.29 us
    all_to_all x1, waiting for transfers between devices, body(): lax.all_to_all(values, 'row', split_axis=0, concat_axis=0, tiled=True)  5.04 us
    ppermute x2, starting transfers between devices, padded_2(): lax.ppermute(tail, axis, [(i, (i + 1) % count) for i in range(ends)])  4.99 us
  transfers between devices with their start and end apart: 9, of which 7 were waited for; matrix products, arithmetic and copies ran while one was open for 13% of the time, Pallas kernels for 0%

commit v1 on v0

v1 whole, which is shorter than its diff:
```python
import functools

import jax
import jax.numpy as jnp
import numpy as np
from jax import lax
from jax.experimental import pallas as pl
from jax.experimental.pallas import tpu as pltpu
from jax.sharding import PartitionSpec as P

LEVELS = 3
STEP = 0.1
SMOOTH_W = 0.5
DATA_W = 20.0
LANES = 128
MESH = pl.DeviceIdType.MESH
F32, BF16, I32 = jnp.float32, jnp.bfloat16, jnp.int32


def haar_pattern(n):
    pattern = np.zeros((n, n), np.float32)
    scale = np.zeros((n,), np.float64)
    cells = np.arange(n)
    base = n >> LEVELS
    for c in range(base):
        pattern[c, cells // 8 == c] = 1.0
        scale[c] = 2.0**-1.5
    for level in range(LEVELS, 0, -1):
        width = 1 << level
        start = n >> level
        for c in range(start):
            inside = cells // width == c
            sign = np.where((cells // (width // 2)) % 2 == 0, 1.0, -1.0)
            pattern[start + c] = np.where(inside, sign, 0.0)
            scale[start + c] = 2.0 ** (-0.5 * level)
    return pattern, scale.astype(np.float32)


def split_hi_lo(value):
    hi = value.astype(BF16)
    lo = (value - hi.astype(F32)).astype(BF16)
    return hi, lo


def dot_nt(a, b):
    return lax.dot_general(a, b, (((1,), (1,)), ((), ())), preferred_element_type=F32)


def dot_nn(a, b):
    return jnp.dot(a, b, preferred_element_type=F32)


def log2(n):
    return n.bit_length() - 1


def kernel(
    dims,
    row_ref,
    owner_ref,
    block_ref,
    obs_ref,
    coef_ref,
    px_ref,
    sx_ref,
    pz_ref,
    pzd_ref,
    szd_ref,
    sens_hbm,
    split_hbm,
    dual_hbm,
    lower_hbm,
    upper_hbm,
    next_ref,
    splitn_ref,
    dualn_ref,
    norm_ref,
    s3,
    split_v,
    dual_v,
    lower_v,
    upper_v,
    ids_all,
    vsend,
    pick_all,
    xs,
    mx_all,
    pred_all,
    contrib2,
    vt,
    v_all,
    model,
    ysend,
    xhalo,
    yhalo,
    zsel,
    norm_row,
    norm_sub,
    local_sem,
    row_send,
    row_recv,
    sub_send,
    sub_recv,
    halo_send,
    halo_recv,
):
    R, S, T, K, NX, NZ, CY, CZ, XL, RB, BLK = dims
    NXB = NX // K
    HALF = T // 2
    HY = LANES // CZ
    Q = CY // HY
    CELLS = XL * CY
    me_r = lax.axis_index("row")
    me_s = lax.axis_index("sub")

    def row_peer(d):
        return {"row": lax.rem(me_r + d, R)}

    def sub_peer(d):
        return {"sub": lax.rem(me_s + d, S)}

    loads = []
    for h in range(2):
        loads.append(
            pltpu.make_async_copy(
                sens_hbm.at[pl.ds(h * HALF, HALF)], s3.at[:, pl.ds(h * K, K), :], local_sem.at[h]
            )
        )
    cell_loads = []
    for n, (src, dst) in enumerate(
        ((split_hbm, split_v), (dual_hbm, dual_v), (lower_hbm, lower_v), (upper_hbm, upper_v))
    ):
        cell_loads.append(pltpu.make_async_copy(src, dst, local_sem.at[2 + n]))

    barrier = pltpu.get_barrier_semaphore()
    for d in range(1, R):
        pl.semaphore_signal(barrier, inc=1, device_id=row_peer(d), device_id_type=MESH)
    for d in range(1, S):
        pl.semaphore_signal(barrier, inc=1, device_id=sub_peer(d), device_id_type=MESH)
    for c in loads + cell_loads:
        c.start()

    gid = owner_ref[...] * BLK + block_ref[...]
    ids_all[me_r] = jnp.broadcast_to(gid, (8, T))
    pl.semaphore_wait(barrier, R - 1 + S - 1)

    def push_row(phase, src_of, dst):
        copies = []
        for d in range(1, R):
            c = pltpu.make_async_remote_copy(
                src_ref=src_of(lax.rem(me_r + d, R)),
                dst_ref=dst.at[me_r],
                send_sem=row_send.at[phase, d - 1],
                recv_sem=row_recv.at[phase, d - 1],
                device_id=row_peer(d),
                device_id_type=MESH,
            )
            c.start()
            copies.append(c)
        return copies

    def push_sub(phase, buf):
        copies = []
        for d in range(1, S):
            c = pltpu.make_async_remote_copy(
                src_ref=buf.at[me_s],
                dst_ref=buf.at[me_s],
                send_sem=sub_send.at[phase, d - 1],
                recv_sem=sub_recv.at[phase, d - 1],
                device_id=sub_peer(d),
                device_id_type=MESH,
            )
            c.start()
            copies.append(c)
        return copies

    sent = push_row(0, lambda r: ids_all.at[me_r], ids_all)

    sx = sx_ref[...]
    for q in range(Q):
        if NX > LANES:
            by_depth = coef_ref[...].reshape(CZ, CY, NX)
            parts = [by_depth[:, h * Q + q, :] for h in range(HY)]
        else:
            parts = [coef_ref[pl.ds(h * Q + q, CZ, stride=CY), :] for h in range(HY)]
        hi, lo = split_hi_lo(jnp.concatenate(parts, axis=0) * sx)
        xs[pl.ds(q, NX, stride=Q), :] = dot_nt(px_ref[...], hi) + dot_nt(px_ref[...], lo)
    low = coef_ref[...].astype(BF16)
    low_twice = []
    for xb in range(NXB):
        part = low[:, xb * K : (xb + 1) * K]
        low_twice.append(jnp.concatenate([part, part], axis=1))
    ZY = BLK // NXB
    lane = lax.broadcasted_iota(I32, (T, LANES), 1)
    first_half = lax.broadcasted_iota(I32, (HALF, LANES), 1) < K
    zy_lane = lax.broadcasted_iota(I32, (T, ZY), 1)
    zc_lane = lax.broadcasted_iota(I32, (T, NZ), 1)
    rows_col = jnp.transpose(jnp.broadcast_to(row_ref[...], (T, T)))
    rows2 = jnp.where(first_half, rows_col[:HALF], rows_col[HALF:])

    own_col = jnp.transpose(jnp.broadcast_to(gid, (T, T)))
    zc_own = lax.shift_right_logical(own_col, log2(CY * NXB))
    z_scale = jnp.where(
        zc_own < NZ // 4,
        2.0**-1.5,
        jnp.where(zc_own < NZ // 2, 0.5, 0.7071067811865476),
    ).astype(F32)
    tile_row_iota = lax.broadcasted_iota(I32, (T, LANES), 0)
    keep = (tile_row_iota < HALF) == (lane < K)
    z_scale = jnp.where(keep, z_scale * (STEP * DATA_W), 0.0)

    for c in sent:
        c.wait()
    cols = []
    for r in range(R):
        col = jnp.transpose(jnp.broadcast_to(ids_all[r, 0:1, :], (T, T)))
        cols.append(col)
        local = col - me_r * BLK
        wide = jnp.concatenate([local] * (ZY // T), axis=1)
        total = None
        for xb in range(NXB):
            hot = jnp.where(wide == zy_lane * NXB + xb, 1.0, 0.0).astype(BF16)
            value = dot_nn(hot, low_twice[xb])
            total = value if total is None else total + value
        vsend[r] = jnp.where(first_half, total[:HALF], total[HALF:]).astype(BF16)
    sent = push_row(1, lambda r: vsend.at[r], pick_all)
    pick_all[me_r] = vsend[me_r]
    bulk = push_row(2, lambda r: xs.at[pl.ds(pl.multiple_of(r * (XL * Q), XL * Q), XL * Q)], mx_all)
    mx_all[me_r] = xs[pl.ds(pl.multiple_of(me_r * (XL * Q), XL * Q), XL * Q), :]

    for r in range(R):
        zc = lax.shift_right_logical(cols[r], log2(CY * NXB))
        zc = jnp.concatenate([zc] * (NZ // T), axis=1)
        hot = jnp.where(zc == zc_lane, 1.0, 0.0).astype(BF16)
        zsel[pl.ds(r * T, T), :] = dot_nn(hot, pz_ref[...]).astype(BF16)

    for c in sent + loads:
        c.wait()
    picked = pick_all[0].astype(F32)
    for r in range(1, R):
        picked = picked + pick_all[r].astype(F32)
    b_iota = lax.broadcasted_iota(I32, (RB, LANES), 0)
    GROUP = 8
    pred = jnp.zeros((RB, T), F32)
    for g in range(HALF // GROUP):
        pieces = []
        for j in range(g * GROUP, (g + 1) * GROUP):
            hit = jnp.broadcast_to(rows2[j : j + 1, :], (RB, LANES)) == b_iota
            pieces.append(jnp.where(hit, jnp.broadcast_to(picked[j : j + 1, :], (RB, LANES)), 0.0))
        left = jnp.concatenate(pieces, axis=1).astype(BF16)
        right = s3[pl.ds(g * GROUP, GROUP)].reshape(GROUP * 2 * K, T)
        pred = pred + dot_nn(left, right)
    pred_all[me_s] = pred
    sent = push_sub(0, pred_all)

    for c in bulk:
        c.wait()
    r_iota = lax.broadcasted_iota(I32, (CELLS, LANES), 0)
    l_iota = lax.broadcasted_iota(I32, (CELLS, LANES), 1)
    own_lane = lax.shift_right_logical(l_iota, log2(CZ)) == lax.shift_right_logical(
        jnp.bitwise_and(r_iota, CY - 1), log2(Q)
    )
    lefts_hi, lefts_lo = [], []
    for r in range(R):
        m = mx_all[r] * szd_ref[r : r + 1, :]
        if Q == 1:
            m = jnp.broadcast_to(m.reshape(XL, 1, LANES), (XL, HY, LANES)).reshape(CELLS, LANES)
        else:
            m = jnp.broadcast_to(m.reshape(XL, 1, Q, LANES), (XL, HY, Q, LANES))
            m = m.reshape(CELLS, LANES)
        hi, lo = split_hi_lo(jnp.where(own_lane, m, 0.0))
        lefts_hi.append(hi)
        lefts_lo.append(lo)
    right = pzd_ref[...]
    now = dot_nn(jnp.concatenate(lefts_hi, axis=1), right) + dot_nn(
        jnp.concatenate(lefts_lo, axis=1), right
    )
    model[pl.ds(8, CELLS), :] = now
    ysend[0] = now.reshape(XL, CY, NZ)[:, 0, :]
    ysend[1] = now.reshape(XL, CY, NZ)[:, CY - 1, :]
    halos = []
    for n, (src, dst, peer) in enumerate(
        (
            (model.at[pl.ds(8, CY)], xhalo.at[1], row_peer(R - 1)),
            (model.at[pl.ds(8 + CELLS - CY, CY)], xhalo.at[0], row_peer(1)),
            (ysend.at[0], yhalo.at[1], sub_peer(S - 1)),
            (ysend.at[1], yhalo.at[0], sub_peer(1)),
        )
    ):
        c = pltpu.make_async_remote_copy(
            src_ref=src,
            dst_ref=dst,
            send_sem=halo_send.at[n],
            recv_sem=halo_recv.at[n],
            device_id=peer,
            device_id_type=MESH,
        )
        c.start()
        halos.append(c)

    for c in sent:
        c.wait()
    predicted = pred_all[0]
    for s in range(1, S):
        predicted = predicted + pred_all[s]
    residual = predicted - obs_ref[...]
    resid_low = residual.astype(BF16)
    for g in range(HALF // GROUP):
        right = s3[pl.ds(g * GROUP, GROUP)].reshape(GROUP * 2 * K, T)
        wide = dot_nt(resid_low, right)
        for n in range(GROUP):
            j = g * GROUP + n
            hit = jnp.broadcast_to(rows2[j : j + 1, :], (RB, LANES)) == b_iota
            piece = jnp.where(hit, wide[:, n * LANES : (n + 1) * LANES], 0.0)
            contrib2[j : j + 1, :] = jnp.sum(piece, axis=0, keepdims=True)
    c2 = contrib2[...]
    scaled = jnp.concatenate([c2, c2], axis=0) * z_scale
    vt_value = None
    for xb in range(NXB):
        part_sx = sx[:, xb * K : (xb + 1) * K]
        part_px = px_ref[:, xb * K : (xb + 1) * K]
        term = scaled * jnp.concatenate([part_sx, part_sx], axis=1)
        if NXB > 1:
            term = jnp.where(jnp.bitwise_and(own_col, NXB - 1) == xb, term, 0.0)
        hi, lo = split_hi_lo(term)
        twice = jnp.concatenate([part_px, part_px], axis=1)
        value = dot_nt(twice, hi) + dot_nt(twice, lo)
        vt_value = value if vt_value is None else vt_value + value
    vt[...] = vt_value
    sent = push_row(3, lambda r: vt.at[pl.ds(pl.multiple_of(r * XL, XL), XL)], v_all)
    v_all[me_r] = vt[pl.ds(pl.multiple_of(me_r * XL, XL), XL), :]

    for c in halos + cell_loads:
        c.wait()
    now = model[pl.ds(8, CELLS), :]
    x_lo = jnp.where(me_r > 0, xhalo[0], 0.0)
    x_hi = jnp.where(me_r < R - 1, xhalo[1], 0.0)
    beside = jnp.concatenate([x_lo, now[: CELLS - CY]], axis=0) + jnp.concatenate(
        [now[CY:], x_hi], axis=0
    )
    y_iota = jnp.bitwise_and(lax.broadcasted_iota(I32, (CELLS, NZ), 0), CY - 1)
    z_iota = lax.broadcasted_iota(I32, (CELLS, NZ), 1)

    def spread(edge):
        return jnp.broadcast_to(edge.reshape(XL, 1, NZ), (XL, CY, NZ)).reshape(CELLS, NZ)

    y_lo = spread(jnp.where(me_s > 0, yhalo[0], 0.0))
    y_hi = spread(jnp.where(me_s < S - 1, yhalo[1], 0.0))
    beside = beside + jnp.where(y_iota == 0, y_lo, pltpu.roll(now, 1, 0))
    beside = beside + jnp.where(y_iota == CY - 1, y_hi, pltpu.roll(now, CELLS - 1, 0))
    beside = beside + jnp.where(z_iota == 0, 0.0, pltpu.roll(now, 1, 1))
    beside = beside + jnp.where(z_iota == NZ - 1, 0.0, pltpu.roll(now, NZ - 1, 1))
    smooth = 6.0 * now - beside
    split_var = split_v[...]
    dual = dual_v[...]
    model[pl.ds(8, CELLS), :] = now - STEP * (SMOOTH_W * smooth + (now - split_var + dual))
    misfit_lane = jnp.sum(residual * residual, axis=0, keepdims=True)

    y_rows = lax.broadcasted_iota(I32, (CY, T), 0)
    y_hits = []
    for r in range(R):
        y_of = jnp.bitwise_and(lax.shift_right_logical(ids_all[r, 0:1, :], log2(NXB)), CY - 1)
        y_hits.append(jnp.where(jnp.broadcast_to(y_of, (CY, T)) == y_rows, 1.0, 0.0))

    for c in sent:
        c.wait()
    his, los = [], []
    for r in range(R):
        w = v_all[r].reshape(XL, 1, T) * y_hits[r].reshape(1, CY, T)
        hi, lo = split_hi_lo(w.reshape(CELLS, T))
        his.append(hi)
        los.append(lo)
    right = zsel[...]
    descent = dot_nn(jnp.concatenate(his, axis=1), right) + dot_nn(
        jnp.concatenate(los, axis=1), right
    )
    model_next = model[pl.ds(8, CELLS), :] - descent
    split_next = jnp.minimum(jnp.maximum(model_next + dual, lower_v[...]), upper_v[...])
    next_ref[...] = model_next
    splitn_ref[...] = split_next
    dualn_ref[...] = dual + model_next - split_next
    gap = model_next - split_next
    move = split_next - split_var
    gap = jnp.sum(gap * gap, axis=0, keepdims=True)
    move = jnp.sum(move * move, axis=0, keepdims=True)
    gap = sum(gap[:, n * LANES : (n + 1) * LANES] for n in range(NZ // LANES))
    move = sum(move[:, n * LANES : (n + 1) * LANES] for n in range(NZ // LANES))
    norm_row[me_r] = jnp.concatenate(
        [misfit_lane, gap, move, jnp.zeros((5, LANES), F32)], axis=0
    )
    for c in push_row(4, lambda r: norm_row.at[me_r], norm_row):
        c.wait()
    total = norm_row[0]
    for r in range(1, R):
        total = total + norm_row[r]
    norm_sub[me_s] = total
    for c in push_sub(1, norm_sub):
        c.wait()
    total = norm_sub[0]
    for s in range(1, S):
        total = total + norm_sub[s]
    total = jnp.broadcast_to(jnp.sum(total, axis=1, keepdims=True), (8, LANES))
    which = lax.broadcasted_iota(I32, (8, LANES), 0)
    cells = CELLS * NZ * R * S
    norm_ref[...] = jnp.where(
        which == 0, total * (0.5 / (RB * T * R * S)), jnp.sqrt(total * (1.0 / cells))
    )


def body(
    observed,
    sens_tiles,
    tile_row,
    tile_owner,
    tile_block,
    coeffs,
    split_var,
    scaled_dual,
    lower_bound,
    upper_bound,
):
    R = lax.axis_size("row")
    S = lax.axis_size("sub")
    T, K = sens_tiles.shape[2], sens_tiles.shape[3]
    CZ, CY, NX = coeffs.shape
    XL, _, NZ = split_var.shape
    RB = observed.shape[0]
    BLK = coeffs.size // K
    HY = LANES // CZ
    Q = CY // HY
    CELLS = XL * CY
    px, sx = haar_pattern(NX)
    pz, sz = haar_pattern(NZ)
    pzd = np.concatenate([np.tile(pz[r * CZ : (r + 1) * CZ], (HY, 1)) for r in range(R)], axis=0)
    szd = np.stack([np.tile(sz[r * CZ : (r + 1) * CZ], HY) for r in range(R)])
    dims = (R, S, T, K, NX, NZ, CY, CZ, XL, RB, BLK)
    vmem = pl.BlockSpec(memory_space=pltpu.VMEM)
    hbm = pl.BlockSpec(memory_space=pl.ANY)
    cell = jax.ShapeDtypeStruct((CELLS, NZ), F32)
    dma = pltpu.SemaphoreType.DMA
    outs = pl.pallas_call(
        functools.partial(kernel, dims),
        out_shape=[cell, cell, cell, jax.ShapeDtypeStruct((8, LANES), F32)],
        in_specs=[vmem] * 10 + [hbm] * 5,
        out_specs=[vmem] * 4,
        scratch_shapes=[
            pltpu.VMEM((T // 2, 2 * K, T), BF16),
            pltpu.VMEM((CELLS, NZ), F32),
            pltpu.VMEM((CELLS, NZ), F32),
            pltpu.VMEM((CELLS, NZ), F32),
            pltpu.VMEM((CELLS, NZ), F32),
            pltpu.VMEM((R, 8, T), I32),
            pltpu.VMEM((R, T // 2, LANES), BF16),
            pltpu.VMEM((R, T // 2, LANES), BF16),
            pltpu.VMEM((NX * Q, LANES), F32),
            pltpu.VMEM((R, XL * Q, LANES), F32),
            pltpu.VMEM((S, RB, T), F32),
            pltpu.VMEM((T // 2, LANES), F32),
            pltpu.VMEM((NX, T), F32),
            pltpu.VMEM((R, XL, T), F32),
            pltpu.VMEM((CELLS + 16, NZ), F32),
            pltpu.VMEM((2, XL, NZ), F32),
            pltpu.VMEM((2, CY, NZ), F32),
            pltpu.VMEM((2, XL, NZ), F32),
            pltpu.VMEM((R * T, NZ), BF16),
            pltpu.VMEM((R, 8, LANES), F32),
            pltpu.VMEM((S, 8, LANES), F32),
            dma((6,)),
            dma((5, R - 1)),
            dma((5, R - 1)),
            dma((2, S - 1)),
            dma((2, S - 1)),
            dma((4,)),
            dma((4,)),
        ],
        compiler_params=pltpu.CompilerParams(
            collective_id=0, has_side_effects=True, vmem_limit_bytes=48 * 1024 * 1024
        ),
        name="admm_step",
    )(
        tile_row.reshape(1, T),
        tile_owner.reshape(1, T),
        tile_block.reshape(1, T),
        observed,
        coeffs.reshape(CZ * CY, NX),
        jnp.asarray(px.T, BF16),
        jnp.asarray(sx[None, :], F32),
        jnp.asarray(pz, BF16),
        jnp.asarray(pzd, BF16),
        jnp.asarray(szd, F32),
        sens_tiles.reshape(T, K, T),
        split_var.reshape(CELLS, NZ),
        scaled_dual.reshape(CELLS, NZ),
        lower_bound.reshape(CELLS, NZ),
        upper_bound.reshape(CELLS, NZ),
    )
    model_next, split_next, dual_next = (o.reshape(split_var.shape) for o in outs[:3])
    return model_next, split_next, dual_next, outs[3][:3, 0]


def solution(mesh):
    in_specs = (
        P(("grp", "row"), None),
        P(("grp", "row"), "sub", None, None, None),
        P(("grp", "row"), "sub", None),
        P(("grp", "row"), "sub", None),
        P(("grp", "row"), "sub", None),
        P(("grp", "row"), "sub", None),
        P(("grp", "row"), "sub", None),
        P(("grp", "row"), "sub", None),
        P(("grp", "row"), "sub", None),
        P(("grp", "row"), "sub", None),
    )
    out_specs = (
        P(("grp", "row"), "sub", None),
        P(("grp", "row"), "sub", None),
        P(("grp", "row"), "sub", None),
        P("grp"),
    )
    return jax.shard_map(body, mesh=mesh, in_specs=in_specs, out_specs=out_specs, check_vma=False)
```

time: 143 us -> 46.1 us (0.32)
  blocking collectives: 43.4 us -> 0 us
  starting transfers between devices: 29.3 us -> 0 us
  Pallas kernels: 0 us -> 29.1 us
  other arithmetic: 18.9 us -> 0 us
  waiting for transfers between devices: 18.6 us -> 0 us
  matrix products: 6.3 us -> 0 us
  local copies, waits for them, and re-layouts: 21 us -> 15.8 us
  between operations: 4.45 us -> 0.67 us
    psum x2 -> x0, blocking collectives: 43.4 us -> none  [the longest x1 33.2 us: body(): primal_sum, dual_sum = lax.psum((primal_part, dual_part), ('row', 'sub'))]
    pallas_call x0 -> x1, Pallas kernels: none -> 29.1 us  [body(): pl.pallas_call(functools.partial(kernel, dims), out_shape=[cell, cell, ce...]
    all_to_all x5 -> x0, starting transfers between devices: 21.7 us -> none  [the longest x1 6.32 us: body(): lax.all_to_all(requests, 'row', split_axis=0, concat_axis=0, tiled=True)]
    all_to_all x5 -> x0, waiting for transfers between devices: 13.2 us -> none  [the longest x1 5.76 us: body(): lax.all_to_all(along_model, 'row', split_axis=2, concat_axis=0, tiled=True)]
    ppermute x4 -> x0, starting transfers between devices: 7.58 us -> none  [the longest x2 4.99 us: padded_2(): lax.ppermute(tail, axis, [(i, (i + 1) % count) for i in range(ends)])]
    all_to_all x6 -> x0, other arithmetic: 6.69 us -> none  [the longest x1 2.28 us: body(): lax.all_to_all(along_grad, 'row', split_axis=2, concat_axis=0, tiled=True)]
    unnamed x27 -> x33, local copies, waits for them, and re-layouts: 9.49 us -> 15.2 us
    all_to_all x8 -> x0, local copies, waits for them, and re-layouts: 5.64 us -> none  [the longest x1 2.19 us: body(): lax.all_to_all(along_grad, 'row', split_axis=2, concat_axis=0, tiled=True)]
  transfers between devices with their start and end apart: 9 -> 0, of which waited for: 7 -> 0; matrix products, arithmetic and copies ran while one was open for 13% -> 0% of each run, Pallas kernels for 0% -> 0%
where the time goes in v1:
time: 46.1 us; the launch traced here: 45.6 us
  Pallas kernels  29.1 us (63%)
  local copies, waits for them, and re-layouts  15.8 us (34%)
  between operations  0.67 us (1%)
    pallas_call x1, Pallas kernels, body(): pl.pallas_call(functools.partial(kernel, dims), out_shape=[cell, cell, ce...  29.1 us
    unnamed x33, local copies, waits for them, and re-layouts  15.2 us

profile of v1, /device:TPU:0, one launch (start us, length us, event | category | flops | bytes accessed | tf_op | source)
XLA Modules:
  0.0 45.6 jit_solution(14053180366622338343)
XLA Ops:
  0.6 0.0 copy-start
  0.6 1.6 %copy-done = bf16[1,1,128,64,128]{4,3,2,1,0:T(8,128)(2,1)S(1)} copy-done((bf16[1,1,128,64,128]{4,3,2,1,0:T(8,128)(2,1)S(1)}, bf16[1,1,128,64,128]{4,3,2,1,0:T(8,128)(2,1)}, u32[]{:S(2)}) %copy-start) | copy-done | bytes 2097176
  2.2 0.0 copy-start.1
  2.2 1.0 %copy-done.1 = f32[64,16,64]{2,1,0:T(8,128)S(1)} copy-done((f32[64,16,64]{2,1,0:T(8,128)S(1)}, f32[64,16,64]{2,1,0:T(8,128)}, u32[]{:S(2)}) %copy-start.1) | copy-done | bytes 262168
  3.3 0.0 copy-start.2
  3.3 0.9 %copy-done.2 = f32[16,16,256]{2,1,0:T(8,128)S(1)} copy-done((f32[16,16,256]{2,1,0:T(8,128)S(1)}, f32[16,16,256]{2,1,0:T(8,128)}, u32[]{:S(2)}) %copy-start.2) | copy-done | bytes 262168
  4.2 0.0 copy-start.3
  4.2 0.9 %copy-done.3 = f32[16,16,256]{2,1,0:T(8,128)S(1)} copy-done((f32[16,16,256]{2,1,0:T(8,128)S(1)}, f32[16,16,256]{2,1,0:T(8,128)}, u32[]{:S(2)}) %copy-start.3) | copy-done | bytes 262168
  5.2 0.0 copy-start.4
  5.2 0.9 %copy-done.4 = f32[16,16,256]{2,1,0:T(8,128)S(1)} copy-done((f32[16,16,256]{2,1,0:T(8,128)S(1)}, f32[16,16,256]{2,1,0:T(8,128)}, u32[]{:S(2)}) %copy-start.4) | copy-done | bytes 262168
  6.1 0.0 copy-start.5
  6.1 0.9 %copy-done.5 = f32[16,16,256]{2,1,0:T(8,128)S(1)} copy-done((f32[16,16,256]{2,1,0:T(8,128)S(1)}, f32[16,16,256]{2,1,0:T(8,128)}, u32[]{:S(2)}) %copy-start.5) | copy-done | bytes 262168
  7.1 0.0 copy-start.6
  7.1 0.9 %copy-done.6 = bf16[512,256]{1,0:T(8,128)(2,1)S(1)} copy-done((bf16[512,256]{1,0:T(8,128)(2,1)S(1)}, bf16[512,256]{1,0:T(8,128)(2,1)}, u32[]{:S(2)}) %copy-start.6) | copy-done | bytes 262168
  8.0 0.0 copy-start.7
  8.0 0.9 %copy-done.7 = bf16[256,256]{1,0:T(8,128)(2,1)S(1)} copy-done((bf16[256,256]{1,0:T(8,128)(2,1)S(1)}, bf16[256,256]{1,0:T(8,128)(2,1)}, u32[]{:S(2)}) %copy-start.7) | copy-done | bytes 131096
  8.9 0.0 copy-start.8
  8.9 0.8 %copy-done.8 = f32[64,128]{1,0:T(8,128)S(1)} copy-done((f32[64,128]{1,0:T(8,128)S(1)}, f32[64,128]{1,0:T(8,128)}, u32[]{:S(2)}) %copy-start.8) | copy-done | bytes 32792
  9.7 0.0 copy-start.9
  9.7 0.7 %copy-done.9 = bf16[64,64]{1,0:T(8,128)(2,1)S(1)} copy-done((bf16[64,64]{1,0:T(8,128)(2,1)S(1)}, bf16[64,64]{1,0:T(8,128)(2,1)}, u32[]{:S(2)}) %copy-start.9) | copy-done | bytes 8216
  10.4 0.0 copy-start.10
  10.4 0.7 %copy-done.10 = f32[4,128]{1,0:T(4,128)S(1)} copy-done((f32[4,128]{1,0:T(4,128)S(1)}, f32[4,128]{1,0:T(4,128)}, u32[]{:S(2)}) %copy-start.10) | copy-done | bytes 2072
  11.1 0.0 copy-start.11
  11.1 0.7 %copy-done.11 = s32[1,1,128]{2,1,0:T(1,128)S(1)} copy-done((s32[1,1,128]{2,1,0:T(1,128)S(1)}, s32[1,1,128]{2,1,0:T(1,128)}, u32[]{:S(2)}) %copy-start.11) | copy-done | bytes 536
  11.7 0.0 copy-start.12
  11.7 0.7 %copy-done.12 = s32[1,1,128]{2,1,0:T(1,128)S(1)} copy-done((s32[1,1,128]{2,1,0:T(1,128)S(1)}, s32[1,1,128]{2,1,0:T(1,128)}, u32[]{:S(2)}) %copy-start.12) | copy-done | bytes 536
  12.4 0.0 copy-start.13
  12.4 0.7 %copy-done.13 = s32[1,1,128]{2,1,0:T(1,128)S(1)} copy-done((s32[1,1,128]{2,1,0:T(1,128)S(1)}, s32[1,1,128]{2,1,0:T(1,128)}, u32[]{:S(2)}) %copy-start.13) | copy-done | bytes 536
  13.1 0.0 copy-start.14
  13.1 0.7 %copy-done.14 = f32[1,64]{1,0:T(1,128)S(1)} copy-done((f32[1,64]{1,0:T(1,128)S(1)}, f32[1,64]{1,0:T(1,128)}, u32[]{:S(2)}) %copy-start.14) | copy-done | bytes 280
  13.7 29.1 %admm_step.1 = (f32[256,256]{1,0:T(8,128)S(1)}, f32[256,256]{1,0:T(8,128)S(1)}, f32[256,256]{1,0:T(8,128)S(1)}, f32[8,128]{1,0:T(8,128)S(1)}) custom-call(s32[1,128]{1,0:T(1,128)S(1)} %bitcast.21, s32[1,128]{1,0:T(1,128)S(1)} %bitcast.22, s32[1,128]{1,0:T(1,128)S(1)} %bitcast.23, f32[64,128]{1,0:T(8,128)S(1)} %copy-done.8, f32[1024,64]{1,0:T(8,128)S(1)} %bitcast.13, ...), custom_call_target="tpu_custom_call" | custom-call | tf_op jit(solution)/shard_map/admm_step/pallas_call | solution.py:441
  42.9 0.6 %slice_reduce_fusion = f32[3]{0:T(128)} fusion(f32[8,128]{1,0:T(8,128)S(1)} %get-tuple-element.11), kind=kLoop, calls=%fused_computation | loop fusion | bytes 24 | tf_op jit(solution)/shard_map/slice | solution.py:498
  43.5 0.7 %copy.22 = f32[16,16,256]{2,1,0:T(8,128)} copy(f32[16,16,256]{2,1,0:T(8,128)S(1)} %bitcast.20) | data formatting | bytes 524288
  44.2 0.7 %copy.23 = f32[16,16,256]{2,1,0:T(8,128)} copy(f32[16,16,256]{2,1,0:T(8,128)S(1)} %bitcast.19) | data formatting | bytes 524288
  44.9 0.7 %copy.24 = f32[16,16,256]{2,1,0:T(8,128)} copy(f32[16,16,256]{2,1,0:T(8,128)S(1)} %bitcast.18) | data formatting | bytes 524288
Async XLA Ops:
  0.6 1.6 %copy-start = (bf16[1,1,128,64,128]{4,3,2,1,0:T(8,128)(2,1)S(1)}, bf16[1,1,128,64,128]{4,3,2,1,0:T(8,128)(2,1)}, u32[]{:S(2)}) copy-start(bf16[1,1,128,64,128]{4,3,2,1,0:T(8,128)(2,1)} %param.16) | copy-start | bytes 6291460
  2.2 1.0 %copy-start.1 = (f32[64,16,64]{2,1,0:T(8,128)S(1)}, f32[64,16,64]{2,1,0:T(8,128)}, u32[]{:S(2)}) copy-start(f32[64,16,64]{2,1,0:T(8,128)} %param.20) | copy-start | bytes 786436
  3.3 0.9 %copy-start.2 = (f32[16,16,256]{2,1,0:T(8,128)S(1)}, f32[16,16,256]{2,1,0:T(8,128)}, u32[]{:S(2)}) copy-start(f32[16,16,256]{2,1,0:T(8,128)} %param.21) | copy-start | bytes 786436
  4.2 0.9 %copy-start.3 = (f32[16,16,256]{2,1,0:T(8,128)S(1)}, f32[16,16,256]{2,1,0:T(8,128)}, u32[]{:S(2)}) copy-start(f32[16,16,256]{2,1,0:T(8,128)} %param.22) | copy-start | bytes 786436
  5.2 0.9 %copy-start.4 = (f32[16,16,256]{2,1,0:T(8,128)S(1)}, f32[16,16,256]{2,1,0:T(8,128)}, u32[]{:S(2)}) copy-start(f32[16,16,256]{2,1,0:T(8,128)} %param.23) | copy-start | bytes 786436
  6.1 0.9 %copy-start.5 = (f32[16,16,256]{2,1,0:T(8,128)S(1)}, f32[16,16,256]{2,1,0:T(8,128)}, u32[]{:S(2)}) copy-start(f32[16,16,256]{2,1,0:T(8,128)} %param.24) | copy-start | bytes 786436
  7.1 0.9 %copy-start.6 = (bf16[512,256]{1,0:T(8,128)(2,1)S(1)}, bf16[512,256]{1,0:T(8,128)(2,1)}, u32[]{:S(2)}) copy-start(bf16[512,256]{1,0:T(8,128)(2,1)} %constant.13.clone.pzd_ref) | copy-start | bytes 786436
  8.0 0.9 %copy-start.7 = (bf16[256,256]{1,0:T(8,128)(2,1)S(1)}, bf16[256,256]{1,0:T(8,128)(2,1)}, u32[]{:S(2)}) copy-start(bf16[256,256]{1,0:T(8,128)(2,1)} %constant.12.clone.pz_ref) | copy-start | bytes 393220
  8.9 0.8 %copy-start.8 = (f32[64,128]{1,0:T(8,128)S(1)}, f32[64,128]{1,0:T(8,128)}, u32[]{:S(2)}) copy-start(f32[64,128]{1,0:T(8,128)} %obs_ref.1) | copy-start | bytes 98308
  9.7 0.7 %copy-start.9 = (bf16[64,64]{1,0:T(8,128)(2,1)S(1)}, bf16[64,64]{1,0:T(8,128)(2,1)}, u32[]{:S(2)}) copy-start(bf16[64,64]{1,0:T(8,128)(2,1)} %constant.10.clone.px_ref) | copy-start | bytes 24580
  10.4 0.7 %copy-start.10 = (f32[4,128]{1,0:T(4,128)S(1)}, f32[4,128]{1,0:T(4,128)}, u32[]{:S(2)}) copy-start(f32[4,128]{1,0:T(4,128)} %constant.14.clone.szd_ref) | copy-start | bytes 6148
  11.1 0.7 %copy-start.11 = (s32[1,1,128]{2,1,0:T(1,128)S(1)}, s32[1,1,128]{2,1,0:T(1,128)}, u32[]{:S(2)}) copy-start(s32[1,1,128]{2,1,0:T(1,128)} %param.17) | copy-start | bytes 1540
  11.7 0.7 %copy-start.12 = (s32[1,1,128]{2,1,0:T(1,128)S(1)}, s32[1,1,128]{2,1,0:T(1,128)}, u32[]{:S(2)}) copy-start(s32[1,1,128]{2,1,0:T(1,128)} %param.18) | copy-start | bytes 1540
  12.4 0.7 %copy-start.13 = (s32[1,1,128]{2,1,0:T(1,128)S(1)}, s32[1,1,128]{2,1,0:T(1,128)}, u32[]{:S(2)}) copy-start(s32[1,1,128]{2,1,0:T(1,128)} %param.19) | copy-start | bytes 1540
  13.1 0.7 %copy-start.14 = (f32[1,64]{1,0:T(1,128)S(1)}, f32[1,64]{1,0:T(1,128)}, u32[]{:S(2)}) copy-start(f32[1,64]{1,0:T(1,128)} %constant.11.clone.sx_ref) | copy-start | bytes 772

commit v2 on v1

--- a/solution.py
+++ b/solution.py
@@ -56,6 +56,23 @@
 
 def kernel(
     dims,
+    row_hbm,
+    owner_hbm,
+    block_hbm,
+    obs_hbm,
+    coef_hbm,
+    px_hbm,
+    sx_hbm,
+    pz_hbm,
+    pzd_hbm,
+    szd_hbm,
+    sens_hbm,
+    split_hbm,
+    dual_hbm,
+    lower_hbm,
+    upper_hbm,
+    shifted_ref,
+    norm_ref,
     row_ref,
     owner_ref,
     block_ref,
@@ -66,15 +83,6 @@
     pz_ref,
     pzd_ref,
     szd_ref,
-    sens_hbm,
-    split_hbm,
-    dual_hbm,
-    lower_hbm,
-    upper_hbm,
-    next_ref,
-    splitn_ref,
-    dualn_ref,
-    norm_ref,
     s3,
     split_v,
     dual_v,
@@ -119,6 +127,24 @@
     def sub_peer(d):
         return {"sub": lax.rem(me_s + d, S)}
 
+    first_loads = []
+    for n, (src, dst) in enumerate(
+        (
+            (owner_hbm, owner_ref),
+            (block_hbm, block_ref),
+            (row_hbm, row_ref),
+            (coef_hbm, coef_ref),
+            (px_hbm, px_ref),
+            (sx_hbm, sx_ref),
+            (pz_hbm, pz_ref),
+            (pzd_hbm, pzd_ref),
+            (szd_hbm, szd_ref),
+            (obs_hbm, obs_ref),
+        )
+    ):
+        first_loads.append(pltpu.make_async_copy(src, dst, local_sem.at[6 + n]))
+        first_loads[-1].start()
+
     loads = []
     for h in range(2):
         loads.append(
@@ -140,6 +166,8 @@
     for c in loads + cell_loads:
         c.start()
 
+    for c in first_loads[:2]:
+        c.wait()
     gid = owner_ref[...] * BLK + block_ref[...]
     ids_all[me_r] = jnp.broadcast_to(gid, (8, T))
     pl.semaphore_wait(barrier, R - 1 + S - 1)
@@ -176,6 +204,8 @@
 
     sent = push_row(0, lambda r: ids_all.at[me_r], ids_all)
 
+    for c in first_loads[2:]:
+        c.wait()
     sx = sx_ref[...]
     for q in range(Q):
         if NX > LANES:
@@ -375,10 +405,8 @@
         jnp.concatenate(los, axis=1), right
     )
     model_next = model[pl.ds(8, CELLS), :] - descent
-    split_next = jnp.minimum(jnp.maximum(model_next + dual, lower_v[...]), upper_v[...])
-    next_ref[...] = model_next
-    splitn_ref[...] = split_next
-    dualn_ref[...] = dual + model_next - split_next
+    shifted = model_next + dual
+    split_next = jnp.minimum(jnp.maximum(shifted, lower_v[...]), upper_v[...])
     gap = model_next - split_next
     move = split_next - split_var
     gap = jnp.sum(gap * gap, axis=0, keepdims=True)
@@ -388,7 +416,9 @@
     norm_row[me_r] = jnp.concatenate(
         [misfit_lane, gap, move, jnp.zeros((5, LANES), F32)], axis=0
     )
-    for c in push_row(4, lambda r: norm_row.at[me_r], norm_row):
+    sent = push_row(4, lambda r: norm_row.at[me_r], norm_row)
+    shifted_ref[...] = shifted
+    for c in sent:
         c.wait()
     total = norm_row[0]
     for r in range(1, R):
@@ -435,15 +465,25 @@
     szd = np.stack([np.tile(sz[r * CZ : (r + 1) * CZ], HY) for r in range(R)])
     dims = (R, S, T, K, NX, NZ, CY, CZ, XL, RB, BLK)
     vmem = pl.BlockSpec(memory_space=pltpu.VMEM)
-    hbm = pl.BlockSpec(memory_space=pl.ANY)
+    hbm = pl.BlockSpec(memory_space=pltpu.HBM)
     cell = jax.ShapeDtypeStruct((CELLS, NZ), F32)
     dma = pltpu.SemaphoreType.DMA
     outs = pl.pallas_call(
         functools.partial(kernel, dims),
-        out_shape=[cell, cell, cell, jax.ShapeDtypeStruct((8, LANES), F32)],
-        in_specs=[vmem] * 10 + [hbm] * 5,
-        out_specs=[vmem] * 4,
+        out_shape=[cell, jax.ShapeDtypeStruct((8, LANES), F32)],
+        in_specs=[hbm] * 15,
+        out_specs=[vmem] * 2,
         scratch_shapes=[
+            pltpu.VMEM((1, T), I32),
+            pltpu.VMEM((1, T), I32),
+            pltpu.VMEM((1, T), I32),
+            pltpu.VMEM((RB, T), F32),
+            pltpu.VMEM((CZ * CY, NX), F32),
+            pltpu.VMEM((NX, NX), BF16),
+            pltpu.VMEM((1, NX), F32),
+            pltpu.VMEM((NZ, NZ), BF16),
+            pltpu.VMEM((R * LANES, NZ), BF16),
+            pltpu.VMEM((R, LANES), F32),
             pltpu.VMEM((T // 2, 2 * K, T), BF16),
             pltpu.VMEM((CELLS, NZ), F32),
             pltpu.VMEM((CELLS, NZ), F32),
@@ -465,7 +505,7 @@
             pltpu.VMEM((R * T, NZ), BF16),
             pltpu.VMEM((R, 8, LANES), F32),
             pltpu.VMEM((S, 8, LANES), F32),
-            dma((6,)),
+            dma((16,)),
             dma((5, R - 1)),
             dma((5, R - 1)),
             dma((2, S - 1)),
@@ -474,7 +514,7 @@
             dma((4,)),
         ],
         compiler_params=pltpu.CompilerParams(
-            collective_id=0, has_side_effects=True, vmem_limit_bytes=48 * 1024 * 1024
+            collective_id=0, has_side_effects=True, vmem_limit_bytes=62 * 1024 * 1024
         ),
         name="admm_step",
     )(
@@ -494,8 +534,11 @@
         lower_bound.reshape(CELLS, NZ),
         upper_bound.reshape(CELLS, NZ),
     )
-    model_next, split_next, dual_next = (o.reshape(split_var.shape) for o in outs[:3])
-    return model_next, split_next, dual_next, outs[3][:3, 0]
+    shifted = outs[0].reshape(split_var.shape)
+    model_next = shifted - scaled_dual
+    split_next = jnp.minimum(jnp.maximum(shifted, lower_bound), upper_bound)
+    dual_next = shifted - split_next
+    return model_next, split_next, dual_next, outs[1][:3, 0]
 
 
 def solution(mesh):

time: 46.1 us -> 34 us (0.74)
  local copies, waits for them, and re-layouts: 15.8 us -> 1.32 us
  other arithmetic: 0 us -> 1.91 us
  Pallas kernels: 29.1 us -> 29.9 us
    unnamed x33 -> x6, local copies, waits for them, and re-layouts: 15.2 us -> 0.01 us
    sub x0 -> x1, other arithmetic: none -> 1.91 us  [body(): dual_next = shifted - split_next]
    pallas_call x1, Pallas kernels: 29.1 us -> 29.9 us  [body(): pl.pallas_call(functools.partial(kernel, dims), out_shape=[cell, jax.Shap...]
    slice x1, local copies, waits for them, and re-layouts: 0.63 us -> 1.31 us  [body(): return (model_next, split_next, dual_next, outs[1][:3, 0])]
where the time goes in v2:
time: 34 us; the launch traced here: 33.8 us
  Pallas kernels  29.9 us (88%)
  other arithmetic  1.91 us (6%)
  local copies, waits for them, and re-layouts  1.32 us (4%)
  between operations  0.67 us (2%)
    pallas_call x1, Pallas kernels, body(): pl.pallas_call(functools.partial(kernel, dims), out_shape=[cell, jax.Shap...  29.9 us
    sub x1, other arithmetic, body(): dual_next = shifted - split_next  1.91 us
    slice x1, local copies, waits for them, and re-layouts, body(): return (model_next, split_next, dual_next, outs[1][:3, 0])  1.31 us

profile of v2, /device:TPU:0, one launch (start us, length us, event | category | flops | bytes accessed | tf_op | source)
XLA Modules:
  0.0 33.8 jit_solution(4750162128173676345)
XLA Ops:
  0.6 0.0 copy-start.2
  0.6 0.0 copy-start.1
  0.7 0.0 copy-start
  0.7 29.9 %admm_step.1 = (f32[256,256]{1,0:T(8,128)}, f32[8,128]{1,0:T(8,128)}) custom-call(s32[1,128]{1,0:T(1,128)} %bitcast.17, s32[1,128]{1,0:T(1,128)} %bitcast.18, s32[1,128]{1,0:T(1,128)} %bitcast.19, f32[64,128]{1,0:T(8,128)} %obs_hbm.1, f32[1024,64]{1,0:T(8,128)} %bitcast.14, bf16[64,64]{1,0:T(8,128)(2,1)} %constant.10.clone.px_hbm, ...), custom_call_target="tpu_custom_call" | custom-call | tf_op jit(solution)/shard_map/admm_step/pallas_call | solution.py:471
  30.6 1.3 %slice_reduce_fusion = f32[3]{0:T(128)} fusion(f32[8,128]{1,0:T(8,128)} %get-tuple-element.7), kind=kLoop, calls=%fused_computation.1 | loop fusion | bytes 24 | tf_op jit(solution)/shard_map/slice | solution.py:541
  31.9 0.0 copy-done.2
  31.9 0.0 copy-done.1
  31.9 0.0 copy-done
  31.9 1.9 %fusion = (f32[16,16,256]{2,1,0:T(8,128)}, f32[16,16,256]{2,1,0:T(8,128)}, f32[16,16,256]{2,1,0:T(8,128)}) fusion(f32[16,16,256]{2,1,0:T(8,128)} %bitcast.16, f32[16,16,256]{2,1,0:T(8,128)S(1)} %copy-done.2, f32[16,16,256]{2,1,0:T(8,128)S(1)} %copy-done.1, f32[16,16,256]{2,1,0:T(8,128)S(1)} %copy-done), kind=kLoop, calls=%fused_computation.2 | loop fusion | flops 262144 | bytes 1835008 | tf_op jit(solution)/shard_map/sub | solution.py:540
Async XLA Ops:
  0.6 31.2 %copy-start.2 = (f32[16,16,256]{2,1,0:T(8,128)S(1)}, f32[16,16,256]{2,1,0:T(8,128)}, u32[]{:S(2)}) copy-start(f32[16,16,256]{2,1,0:T(8,128)} %param.24) | copy-start | bytes 786436
  0.6 31.2 %copy-start.1 = (f32[16,16,256]{2,1,0:T(8,128)S(1)}, f32[16,16,256]{2,1,0:T(8,128)}, u32[]{:S(2)}) copy-start(f32[16,16,256]{2,1,0:T(8,128)} %param.23) | copy-start | bytes 786436
  0.7 31.2 %copy-start = (f32[16,16,256]{2,1,0:T(8,128)S(1)}, f32[16,16,256]{2,1,0:T(8,128)}, u32[]{:S(2)}) copy-start(f32[16,16,256]{2,1,0:T(8,128)} %param.22) | copy-start | bytes 786436

commit v3 on v2

--- a/solution.py
+++ b/solution.py
@@ -104,6 +104,7 @@
     zsel,
     norm_row,
     norm_sub,
+    norm_all,
     local_sem,
     row_send,
     row_recv,
@@ -111,6 +112,8 @@
     sub_recv,
     halo_send,
     halo_recv,
+    norm_send,
+    norm_recv,
 ):
     R, S, T, K, NX, NZ, CY, CZ, XL, RB, BLK = dims
     NXB = NX // K
@@ -159,18 +162,22 @@
         cell_loads.append(pltpu.make_async_copy(src, dst, local_sem.at[2 + n]))
 
     barrier = pltpu.get_barrier_semaphore()
-    for d in range(1, R):
-        pl.semaphore_signal(barrier, inc=1, device_id=row_peer(d), device_id_type=MESH)
-    for d in range(1, S):
-        pl.semaphore_signal(barrier, inc=1, device_id=sub_peer(d), device_id_type=MESH)
+    direct = R * S <= 16
+    if direct:
+        all_peers = [
+            {**row_peer(d), **sub_peer(e)} for d in range(R) for e in range(S) if d + e > 0
+        ]
+    near = [row_peer(d) for d in range(1, R)] + [sub_peer(d) for d in range(1, S)]
+    for peer in near:
+        pl.semaphore_signal(barrier, inc=1, device_id=peer, device_id_type=MESH)
     for c in loads + cell_loads:
         c.start()
 
     for c in first_loads[:2]:
         c.wait()
     gid = owner_ref[...] * BLK + block_ref[...]
-    ids_all[me_r] = jnp.broadcast_to(gid, (8, T))
-    pl.semaphore_wait(barrier, R - 1 + S - 1)
+    ids_all[me_r] = gid
+    pl.semaphore_wait(barrier, len(near))
 
     def push_row(phase, src_of, dst):
         copies = []
@@ -215,6 +222,8 @@
             parts = [coef_ref[pl.ds(h * Q + q, CZ, stride=CY), :] for h in range(HY)]
         hi, lo = split_hi_lo(jnp.concatenate(parts, axis=0) * sx)
         xs[pl.ds(q, NX, stride=Q), :] = dot_nt(px_ref[...], hi) + dot_nt(px_ref[...], lo)
+    bulk = push_row(2, lambda r: xs.at[pl.ds(pl.multiple_of(r * (XL * Q), XL * Q), XL * Q)], mx_all)
+    mx_all[me_r] = xs[pl.ds(pl.multiple_of(me_r * (XL * Q), XL * Q), XL * Q), :]
     low = coef_ref[...].astype(BF16)
     low_twice = []
     for xb in range(NXB):
@@ -255,33 +264,6 @@
         vsend[r] = jnp.where(first_half, total[:HALF], total[HALF:]).astype(BF16)
     sent = push_row(1, lambda r: vsend.at[r], pick_all)
     pick_all[me_r] = vsend[me_r]
-    bulk = push_row(2, lambda r: xs.at[pl.ds(pl.multiple_of(r * (XL * Q), XL * Q), XL * Q)], mx_all)
-    mx_all[me_r] = xs[pl.ds(pl.multiple_of(me_r * (XL * Q), XL * Q), XL * Q), :]
-
-    for r in range(R):
-        zc = lax.shift_right_logical(cols[r], log2(CY * NXB))
-        zc = jnp.concatenate([zc] * (NZ // T), axis=1)
-        hot = jnp.where(zc == zc_lane, 1.0, 0.0).astype(BF16)
-        zsel[pl.ds(r * T, T), :] = dot_nn(hot, pz_ref[...]).astype(BF16)
-
-    for c in sent + loads:
-        c.wait()
-    picked = pick_all[0].astype(F32)
-    for r in range(1, R):
-        picked = picked + pick_all[r].astype(F32)
-    b_iota = lax.broadcasted_iota(I32, (RB, LANES), 0)
-    GROUP = 8
-    pred = jnp.zeros((RB, T), F32)
-    for g in range(HALF // GROUP):
-        pieces = []
-        for j in range(g * GROUP, (g + 1) * GROUP):
-            hit = jnp.broadcast_to(rows2[j : j + 1, :], (RB, LANES)) == b_iota
-            pieces.append(jnp.where(hit, jnp.broadcast_to(picked[j : j + 1, :], (RB, LANES)), 0.0))
-        left = jnp.concatenate(pieces, axis=1).astype(BF16)
-        right = s3[pl.ds(g * GROUP, GROUP)].reshape(GROUP * 2 * K, T)
-        pred = pred + dot_nn(left, right)
-    pred_all[me_s] = pred
-    sent = push_sub(0, pred_all)
 
     for c in bulk:
         c.wait()
@@ -327,6 +309,37 @@
         )
         c.start()
         halos.append(c)
+
+    for c in sent + loads:
+        c.wait()
+    picked = pick_all[0].astype(F32)
+    for r in range(1, R):
+        picked = picked + pick_all[r].astype(F32)
+    b_iota = lax.broadcasted_iota(I32, (RB, LANES), 0)
+    GROUP = 8
+    pred = jnp.zeros((RB, T), F32)
+    for g in range(HALF // GROUP):
+        pieces = []
+        for j in range(g * GROUP, (g + 1) * GROUP):
+            hit = jnp.broadcast_to(rows2[j : j + 1, :], (RB, LANES)) == b_iota
+            pieces.append(jnp.where(hit, jnp.broadcast_to(picked[j : j + 1, :], (RB, LANES)), 0.0))
+        left = jnp.concatenate(pieces, axis=1).astype(BF16)
+        right = s3[pl.ds(g * GROUP, GROUP)].reshape(GROUP * 2 * K, T)
+        pred = pred + dot_nn(left, right)
+    pred_all[me_s] = pred
+    sent = push_sub(0, pred_all)
+
+    for r in range(R):
+        zc = lax.shift_right_logical(cols[r], log2(CY * NXB))
+        zc = jnp.concatenate([zc] * (NZ // T), axis=1)
+        hot = jnp.where(zc == zc_lane, 1.0, 0.0).astype(BF16)
+        zsel[pl.ds(r * T, T), :] = dot_nn(hot, pz_ref[...]).astype(BF16)
+
+    y_rows = lax.broadcasted_iota(I32, (CY, T), 0)
+    y_hits = []
+    for r in range(R):
+        y_of = jnp.bitwise_and(lax.shift_right_logical(ids_all[r, 0:1, :], log2(NXB)), CY - 1)
+        y_hits.append(jnp.where(jnp.broadcast_to(y_of, (CY, T)) == y_rows, 1.0, 0.0))
 
     for c in sent:
         c.wait()
@@ -384,13 +397,8 @@
     split_var = split_v[...]
     dual = dual_v[...]
     model[pl.ds(8, CELLS), :] = now - STEP * (SMOOTH_W * smooth + (now - split_var + dual))
+
     misfit_lane = jnp.sum(residual * residual, axis=0, keepdims=True)
-
-    y_rows = lax.broadcasted_iota(I32, (CY, T), 0)
-    y_hits = []
-    for r in range(R):
-        y_of = jnp.bitwise_and(lax.shift_right_logical(ids_all[r, 0:1, :], log2(NXB)), CY - 1)
-        y_hits.append(jnp.where(jnp.broadcast_to(y_of, (CY, T)) == y_rows, 1.0, 0.0))
 
     for c in sent:
         c.wait()
@@ -411,30 +419,63 @@
     move = split_next - split_var
     gap = jnp.sum(gap * gap, axis=0, keepdims=True)
     move = jnp.sum(move * move, axis=0, keepdims=True)
-    gap = sum(gap[:, n * LANES : (n + 1) * LANES] for n in range(NZ // LANES))
-    move = sum(move[:, n * LANES : (n + 1) * LANES] for n in range(NZ // LANES))
-    norm_row[me_r] = jnp.concatenate(
-        [misfit_lane, gap, move, jnp.zeros((5, LANES), F32)], axis=0
-    )
-    sent = push_row(4, lambda r: norm_row.at[me_r], norm_row)
-    shifted_ref[...] = shifted
-    for c in sent:
-        c.wait()
-    total = norm_row[0]
-    for r in range(1, R):
-        total = total + norm_row[r]
-    norm_sub[me_s] = total
-    for c in push_sub(1, norm_sub):
-        c.wait()
-    total = norm_sub[0]
-    for s in range(1, S):
-        total = total + norm_sub[s]
-    total = jnp.broadcast_to(jnp.sum(total, axis=1, keepdims=True), (8, LANES))
-    which = lax.broadcasted_iota(I32, (8, LANES), 0)
+    one = lax.broadcasted_iota(I32, (1, LANES), 1)
+    sums = jnp.where(
+        one == 0,
+        jnp.sum(misfit_lane, axis=1, keepdims=True),
+        jnp.where(
+            one == 1, jnp.sum(gap, axis=1, keepdims=True), jnp.sum(move, axis=1, keepdims=True)
+        ),
+    )
+    if direct:
+        norm_all[me_r * S + me_s] = sums
+        sent = []
+        for n, peer in enumerate(all_peers):
+            c = pltpu.make_async_remote_copy(
+                src_ref=norm_all.at[me_r * S + me_s],
+                dst_ref=norm_all.at[me_r * S + me_s],
+                send_sem=norm_send.at[n],
+                recv_sem=norm_recv.at[n],
+                device_id=peer,
+                device_id_type=MESH,
+            )
+            c.start()
+            sent.append(c)
+        shifted_ref[...] = shifted
+        for c in sent:
+            c.wait()
+        total = norm_all[0]
+        for n in range(1, R * S):
+            total = total + norm_all[n]
+    else:
+        norm_row[me_r] = sums
+        sent = push_row(4, lambda r: norm_row.at[me_r], norm_row)
+        shifted_ref[...] = shifted
+        for c in sent:
+            c.wait()
+        total = norm_row[0]
+        for r in range(1, R):
+            total = total + norm_row[r]
+        norm_sub[me_s] = total
+        for c in push_sub(1, norm_sub):
+            c.wait()
+        total = norm_sub[0]
+        for s in range(1, S):
+            total = total + norm_sub[s]
     cells = CELLS * NZ * R * S
     norm_ref[...] = jnp.where(
-        which == 0, total * (0.5 / (RB * T * R * S)), jnp.sqrt(total * (1.0 / cells))
-    )
+        one == 0, total * (0.5 / (RB * T * R * S)), jnp.sqrt(total * (1.0 / cells))
+    )
+
+
+def finish(shifted_ref, dual_ref, lower_ref, upper_ref, norm_ref, next_ref, split_ref, out_ref, norms_ref):
+    shifted = shifted_ref[...]
+    split_next = jnp.minimum(jnp.maximum(shifted, lower_ref[...]), upper_ref[...])
+    next_ref[...] = shifted - dual_ref[...]
+    split_ref[...] = split_next
+    out_ref[...] = shifted - split_next
+    for n in range(3):
+        norms_ref[n] = norm_ref[0, n]
 
 
 def body(
@@ -470,7 +511,7 @@
     dma = pltpu.SemaphoreType.DMA
     outs = pl.pallas_call(
         functools.partial(kernel, dims),
-        out_shape=[cell, jax.ShapeDtypeStruct((8, LANES), F32)],
+        out_shape=[cell, jax.ShapeDtypeStruct((1, LANES), F32)],
         in_specs=[hbm] * 15,
         out_specs=[vmem] * 2,
         scratch_shapes=[
@@ -489,7 +530,7 @@
             pltpu.VMEM((CELLS, NZ), F32),
             pltpu.VMEM((CELLS, NZ), F32),
             pltpu.VMEM((CELLS, NZ), F32),
-            pltpu.VMEM((R, 8, T), I32),
+            pltpu.VMEM((R, 1, T), I32),
             pltpu.VMEM((R, T // 2, LANES), BF16),
             pltpu.VMEM((R, T // 2, LANES), BF16),
             pltpu.VMEM((NX * Q, LANES), F32),
@@ -503,8 +544,9 @@
             pltpu.VMEM((2, CY, NZ), F32),
             pltpu.VMEM((2, XL, NZ), F32),
             pltpu.VMEM((R * T, NZ), BF16),
-            pltpu.VMEM((R, 8, LANES), F32),
-            pltpu.VMEM((S, 8, LANES), F32),
+            pltpu.VMEM((R, 1, LANES), F32),
+            pltpu.VMEM((S, 1, LANES), F32),
+            pltpu.VMEM((R * S, 1, LANES), F32),
             dma((16,)),
             dma((5, R - 1)),
             dma((5, R - 1)),
@@ -512,6 +554,8 @@
             dma((2, S - 1)),
             dma((4,)),
             dma((4,)),
+            dma((R * S - 1,)),
+            dma((R * S - 1,)),
         ],
         compiler_params=pltpu.CompilerParams(
             collective_id=0, has_side_effects=True, vmem_limit_bytes=62 * 1024 * 1024
@@ -534,11 +578,22 @@
         lower_bound.reshape(CELLS, NZ),
         upper_bound.reshape(CELLS, NZ),
     )
-    shifted = outs[0].reshape(split_var.shape)
-    model_next = shifted - scaled_dual
-    split_next = jnp.minimum(jnp.maximum(shifted, lower_bound), upper_bound)
-    dual_next = shifted - split_next
-    return model_next, split_next, dual_next, outs[1][:3, 0]
+    smem = pl.BlockSpec(memory_space=pltpu.SMEM)
+    model_next, split_next, dual_next, norms = pl.pallas_call(
+        finish,
+        out_shape=[cell, cell, cell, jax.ShapeDtypeStruct((3,), F32)],
+        in_specs=[vmem] * 4 + [smem],
+        out_specs=[vmem] * 3 + [smem],
+        name="cell_outputs",
+    )(
+        outs[0],
+        scaled_dual.reshape(CELLS, NZ),
+        lower_bound.reshape(CELLS, NZ),
+        upper_bound.reshape(CELLS, NZ),
+        outs[1],
+    )
+    shape = split_var.shape
+    return model_next.reshape(shape), split_next.reshape(shape), dual_next.reshape(shape), norms
 
 
 def solution(mesh):

time: 34 us -> 31.2 us (0.918)
  other arithmetic: 1.91 us -> 0 us
  local copies, waits for them, and re-layouts: 1.32 us -> 0 us
  Pallas kernels: 29.9 us -> 30.4 us
    pallas_call x0 -> x1, Pallas kernels: none -> 2.13 us  [body(): pl.pallas_call(finish, out_shape=[cell, cell, cell, jax.ShapeDtypeStruct(...]
    sub x1 -> x0, other arithmetic: 1.91 us -> none  [body(): dual_next = shifted - split_next]
    pallas_call x1, Pallas kernels: 29.9 us -> 28.2 us  [body(): pl.pallas_call(functools.partial(kernel, dims), out_shape=[cell, jax.Shap...]
    slice x1 -> x0, local copies, waits for them, and re-layouts: 1.31 us -> none  [body(): return (model_next, split_next, dual_next, outs[1][:3, 0])]
where the time goes in v3:
time: 31.2 us; the launch traced here: 31 us
  Pallas kernels  30.4 us (97%)
  between operations  0.64 us (2%)
    pallas_call x1, Pallas kernels, body(): pl.pallas_call(functools.partial(kernel, dims), out_shape=[cell, jax.Shap...  28.2 us
    pallas_call x1, Pallas kernels, body(): pl.pallas_call(finish, out_shape=[cell, cell, cell, jax.ShapeDtypeStruct(...  2.13 us

profile of v3, /device:TPU:0, one launch (start us, length us, event | category | flops | bytes accessed | tf_op | source)
XLA Modules:
  0.0 31.0 jit_solution(11552148196420713287)
XLA Ops:
  0.6 28.2 %admm_step.1 = (f32[256,256]{1,0:T(8,128)}, f32[1,128]{1,0:T(1,128)}) custom-call(s32[1,128]{1,0:T(1,128)} %bitcast.21, s32[1,128]{1,0:T(1,128)} %bitcast.22, s32[1,128]{1,0:T(1,128)} %bitcast.23, f32[64,128]{1,0:T(8,128)} %obs_hbm.1, f32[1024,64]{1,0:T(8,128)} %bitcast.19, bf16[64,64]{1,0:T(8,128)(2,1)} %constant.10.clone.px_hbm, ...), custom_call_target="tpu_custom_call" | custom-call | tf_op jit(solution)/shard_map/admm_step/pallas_call | solution.py:512
  28.9 2.1 %cell_outputs.1 = (f32[256,256]{1,0:T(8,128)}, f32[256,256]{1,0:T(8,128)}, f32[256,256]{1,0:T(8,128)}, f32[3]{0:T(128)}) custom-call(f32[256,256]{1,0:T(8,128)} %get-tuple-element.10.shifted_ref, f32[256,256]{1,0:T(8,128)} %bitcast.14, f32[256,256]{1,0:T(8,128)} %bitcast.16, f32[256,256]{1,0:T(8,128)} %bitcast.18, f32[1,128]{1,0:T(1,128)} %get-tuple-element.11.norm_ref), custom_call_target="tpu_custom_call" | custom-call | tf_op jit(solution)/shard_map/cell_outputs/pallas_call | solution.py:582
